TPU v7x, 32 devices: a whole 2x2x4 slice. The times are simulated.
32 devices in a mesh: groups: 2 (over y), ctx: 4 (over z), tp: 4 (over x, core).
Axes of the slice: x: 2, y: 2, z: 4, core: 2. Of those that a mesh axis runs over, the one named last changes fastest.
Arguments:
- queries: bfloat16 [2048, 4096], P(('groups', 'ctx'), 'tp'), parts along dimension 0, may hold values from -24 to 24
- response_keys: bfloat16 [2048, 512], P(('groups', 'ctx'), 'tp'), parts along dimension 0, may hold values from -4.5 to 4.5
- response_values: bfloat16 [2048, 512], P(('groups', 'ctx'), 'tp'), parts along dimension 0, may hold values from -6 to 6
- prompt_keys: bfloat16 [2048, 512], P(('groups', 'ctx'), 'tp'), parts along dimension 0, may hold values from -4.5 to 4.5
- prompt_values: bfloat16 [2048, 512], P(('groups', 'ctx'), 'tp'), parts along dimension 0, may hold values from -6 to 6
- response_lengths: int32 [12], P('groups'), parts along dimension 0, may hold values from 1 to 256, 1024 in all
- out_weight: bfloat16 [4096, 4096], P('tp'), may hold values from -0.75 to 0.75
Outputs:
- projected: bfloat16 [2048, 4096], P(('groups', 'ctx'), 'tp'), parts along dimension 0
There are 2 independent parts, one for each index of `groups`. A program takes and returns all parts, laid end to end along the dimension named above; an argument that names none is the same for every part. Nothing has to cross between parts.
Inputs may be any that keep to these rules, and one draw needn't show every extreme that they name: `response_lengths`: they sum to 1024; the longest is exactly 256.
All inputs are finite; a program needn't handle non-finite values.
Results may differ from a plain program's by a relative error of at most 0.013.
Values may be sent and summed in bfloat16 or wider, within the bound.
A program may use at most 64 MiB of HBM per device.

v0:
```python
import jax
import jax.numpy as jnp
from jax import lax
from jax.sharding import PartitionSpec as P

HD = 128
LEN_MAX = 256


def shifted(block, axis, distance):
    devices = range(lax.axis_size(axis))
    route = [(i - distance, i) for i in devices if i - distance in devices]
    return lax.ppermute(block, axis, route)


def block_stats(query_rows, keys, values, allowed):
    kv_local = query_rows.shape[1]
    count = keys.shape[0]
    keys = keys.reshape(count, kv_local, HD)
    values = values.reshape(count, kv_local, HD)
    scores = jnp.einsum("rkgd,skd->kgrs", query_rows, keys, preferred_element_type=jnp.float32) * (
        1.0 / HD**0.5
    )
    if allowed is not None:
        scores = jnp.where(allowed, scores, -jnp.inf)
    top = jnp.max(scores, axis=-1)
    weights = jnp.exp(scores - top[..., None])
    total = jnp.sum(weights, axis=-1)
    summed = jnp.einsum(
        "kgrs,skd->kgrd", weights.astype(jnp.bfloat16), values, preferred_element_type=jnp.float32
    )
    return (top, total, summed)


def combine_stats(first, second):
    top = jnp.maximum(first[0], second[0])
    first_scale = jnp.exp(first[0] - top)
    second_scale = jnp.exp(second[0] - top)
    total = first[1] * first_scale + second[1] * second_scale
    summed = first[2] * first_scale[..., None] + second[2] * second_scale[..., None]
    return (top, total, summed)


def local(
    queries,
    response_keys,
    response_values,
    prompt_keys,
    prompt_values,
    response_lengths,
    out_weight,
):
    rows, query_cols = queries.shape
    kv_cols = response_keys.shape[1]
    kv_local = kv_cols // HD
    group = query_cols // kv_cols
    query_rows = queries.reshape(rows, kv_local, group, HD)
    previous = shifted(jnp.stack([response_keys, response_values]), "ctx", 1)
    both_k = jnp.concatenate([previous[0], response_keys], axis=0)
    both_v = jnp.concatenate([previous[1], response_values], axis=0)
    base = lax.axis_index("ctx") * rows
    positions = base + jnp.arange(rows, dtype=jnp.int32)
    starts = jnp.cumsum(response_lengths) - response_lengths
    first = jnp.max(jnp.where(starts[None, :] <= positions[:, None], starts[None, :], 0), axis=1)
    block = min(rows, 512)
    window = LEN_MAX + block

    def self_block(index):
        begin = index * block
        key_begin = rows + begin - LEN_MAX
        key_pos = base - rows + key_begin + jnp.arange(window, dtype=jnp.int32)
        allowed = (key_pos[None, :] >= first[:, None]) & (key_pos[None, :] <= positions[:, None])
        return block_stats(query_rows, both_k, both_v, allowed)

    tops, totals, sums = lax.map(self_block, jnp.arange(rows // block, dtype=jnp.int32))
    tops = jnp.transpose(tops, (1, 2, 0, 3)).reshape(kv_local, group, rows)
    totals = jnp.transpose(totals, (1, 2, 0, 3)).reshape(kv_local, group, rows)
    sums = jnp.transpose(sums, (1, 2, 0, 3, 4)).reshape(kv_local, group, rows, HD)
    carry = (tops, totals, sums)
    piece_k = lax.all_gather(prompt_keys, "ctx", axis=0, tiled=True)
    piece_v = lax.all_gather(prompt_values, "ctx", axis=0, tiled=True)
    count = piece_k.shape[0]

    def step(state, pair):
        return (combine_stats(state, block_stats(query_rows, pair[0], pair[1], None)), None)

    blocks_k = piece_k.reshape(count // 512, 512, kv_cols)
    blocks_v = piece_v.reshape(count // 512, 512, kv_cols)
    carry, unused = lax.scan(step, carry, (blocks_k, blocks_v))
    attended = carry[2] / carry[1][..., None]
    attended = jnp.transpose(attended, (2, 0, 1, 3)).reshape(rows, query_cols).astype(jnp.bfloat16)
    partial_value = jnp.dot(attended, out_weight, preferred_element_type=jnp.float32)
    return lax.psum_scatter(
        partial_value.astype(jnp.bfloat16), "tp", scatter_dimension=1, tiled=True
    )


def solution(mesh):
    placed = (
        P(("groups", "ctx"), "tp"),
        P(("groups", "ctx"), "tp"),
        P(("groups", "ctx"), "tp"),
        P(("groups", "ctx"), "tp"),
        P(("groups", "ctx"), "tp"),
        P("groups"),
        P("tp", None),
    )
    return jax.shard_map(
        local, mesh=mesh, in_specs=placed, out_specs=P(("groups", "ctx"), "tp"), check_vma=False
    )
```

profile of v0, /device:TPU:0, one launch (start us, length us, event | category | flops | bytes accessed | tf_op | source)
XLA Modules:
  0.0 99.8 jit_solution(16345644374997361708)
XLA Ops:
  6.5 0.0 reduce-scatter.2.cloned.1.call-start
  6.5 0.9 pad_maximum_fusion
  7.4 4.9 %collective-permute-start = (bf16[2,256,128]{2,1,0:T(8,128)(2,1)S(1)}, bf16[2,256,128]{2,1,0:T(8,128)(2,1)S(1)}, u32[]{:S(2)}, u32[]{:S(2)}) collective-permute-start(bf16[2,256,128]{2,1,0:T(8,128)(2,1)S(1)} %pad_maximum_fusion), channel_id=1, source_target_pairs={{0,4},{4,8},{8,12},{1,5},{5,9},{9,13},{2,6},{6,10},{10,14},{3,7},{... | collective-permute-start | bytes 393224 | tf_op jit(solution)/shard_map/ppermute | solution.py:13
  12.4 0.8 reduce-window.9
  13.2 0.7 bitcast_subtract_fusion.2
  13.9 0.1 select_reduce_fusion
  14.0 0.2 compare_and_fusion
  14.1 15.0 %all_gather.6 = bf16[1024,128]{1,0:T(8,128)(2,1)S(1)} all-gather(bf16[256,128]{1,0:T(8,128)(2,1)} %param.12), channel_id=1, replica_groups=mesh['groups'=2,'ctx'=4,'tp'=4] {'ctx'}, dimensions={0}, use_global_device_ids=true | all-gather | bytes 327680 | tf_op jit(solution)/shard_map/all_gather | solution.py:80
  29.1 1.2 %copy.20 = bf16[256,1024]{0,1:T(8,128)(2,1)S(1)} copy(bf16[256,1024]{1,0:T(8,128)(2,1)} %param.9) | data formatting | bytes 1048576 | tf_op args[0]
  30.3 0.3 copy.21
  30.6 14.4 %all_gather.7 = bf16[1024,128]{1,0:T(8,128)(2,1)S(1)} all-gather(bf16[256,128]{1,0:T(8,128)(2,1)} %param.13), channel_id=1, replica_groups=mesh['groups'=2,'ctx'=4,'tp'=4] {'ctx'}, dimensions={0}, use_global_device_ids=true | all-gather | bytes 327680 | tf_op jit(solution)/shard_map/all_gather | solution.py:81
  45.0 0.0 collective-permute-done
  45.0 0.0 copy-start
  45.0 1.9 %fusion.32 = (f32[8,256]{1,0:T(8,128)S(1)}, f32[512,256,8]{1,0,2:T(8,128)S(1)}) fusion(pred[256,512]{0,1:T(8,128)(4,1)S(1)} %compare_and_fusion, bf16[256,128]{1,0:T(8,128)(2,1)} %param.10, bf16[256,128]{1,0:T(8,128)(2,1)S(1)} %get-tuple-element.110, bf16[256,1024]{1,0:T(8,128)(2,1)} %param.9), kind=kOutput, calls=%fused_computation.34 | convolution fusion | flops 271841280 | bytes 4988928 | tf_op jit(solution)/shard_map/while/body/eval_jaxpr/rkgd,skd->kgrs/dot_general | solution.py:21
  46.9 0.9 fusion.31
  47.8 0.0 copy-done
  47.8 1.2 %fusion.37 = f32[1,8,256,128]{3,2,1,0:T(8,128)S(1)} fusion(f32[512,256,8]{1,0,2:T(8,128)S(1)} %get-tuple-element.112, f32[8,256]{1,0:T(8,128)S(1)} %get-tuple-element.111, pred[256,512]{0,1:T(8,128)(4,1)S(1)} %compare_and_fusion, bf16[256,128]{1,0:T(8,128)(2,1)S(1)} %copy-done, bf16[256,128]{1,0:T(8,128)(2,1)S(1)} %get-tuple-element.109), kind=kOutput, calls=%fused_computation.38 | convolution fusion | flops 272891904 | bytes 5513216 | tf_op jit(solution)/shard_map/while/body/eval_jaxpr/kgrs,skd->kgrd/dot_general | solution.py:29
  49.0 6.4 %while.2 = (s32[]{:T(128)}, f32[1,8,256]{2,1,0:T(8,128)S(1)}, f32[1,8,256]{2,1,0:T(8,128)S(1)}, f32[1,8,256,128]{3,2,1,0:T(8,128)S(1)}, bf16[2,512,128]{2,1,0:T(...) while((s32[]{:T(128)}, f32[1,8,256]{2,1,0:T(8,128)S(1)}, ...), condition=%wide.region_7.8_spmd, body=%wide.region_4.7_spmd.sunk | while | flops 546056192 | bytes 15622237 | solution.py:89
  49.0 0.7 bitcast_reduce_fusion.2
  49.7 0.7 fusion.63
  50.5 1.7 %fusion.65 = f32[1,8,256,128]{3,2,1,0:T(8,128)S(1)} fusion(f32[512,256,8]{1,0,2:T(8,128)S(1)} %get-tuple-element.164, f32[8,256]{1,0:T(8,128)S(1)} %get-tuple-element.162, f32[1,8,256,128]{3,2,1,0:T(8,128)S(1)} %get-tuple-element.179, f32[8,256]{1,0:T(8,128)S(1)} %get-tuple-element.166, f32[8,256]{1,0:T(8,128)S(1)} %get-tuple-element.167, ...), kind=kOutput, calls=%fused_computation.11.clone.1 | convolution fusion | flops 272367616 | bytes 6447108 | tf_op jit(solution)/shard_map/while/body/eval_jaxpr/kgrs,skd->kgrd/dot_general | solution.py:29
  52.2 0.7 bitcast_reduce_fusion.2
  52.9 0.7 fusion.63
  53.7 1.7 %fusion.65 = f32[1,8,256,128]{3,2,1,0:T(8,128)S(1)} fusion(f32[512,256,8]{1,0,2:T(8,128)S(1)} %get-tuple-element.164, f32[8,256]{1,0:T(8,128)S(1)} %get-tuple-element.162, f32[1,8,256,128]{3,2,1,0:T(8,128)S(1)} %get-tuple-element.179, f32[8,256]{1,0:T(8,128)S(1)} %get-tuple-element.166, f32[8,256]{1,0:T(8,128)S(1)} %get-tuple-element.167, ...), kind=kOutput, calls=%fused_computation.11.clone.1 | convolution fusion | flops 272367616 | bytes 6447108 | tf_op jit(solution)/shard_map/while/body/eval_jaxpr/kgrs,skd->kgrd/dot_general | solution.py:29
  55.4 0.3 copy.22
  55.8 0.1 divide_convert_fusion
  55.9 7.1 %convolution_convert_fusion = bf16[256,4096]{1,0:T(8,128)(2,1)} fusion(bf16[256,1024]{0,1:T(8,128)(2,1)S(1)} %bitcast.149, bf16[1024,4096]{1,0:T(8,128)(2,1)} %param.15), kind=kOutput, calls=%fused_computation.29 | convolution fusion | flops 2148532224 | bytes 11010048 | tf_op jit(solution)/shard_map/dot_general | solution.py:92
  63.0 0.0 reduce-scatter.2.cloned.1.call-update
  63.0 29.9 %reduce-scatter.2.cloned.1.call-done = bf16[256,1024]{1,0:T(8,128)(2,1)} async-done(((bf16[256,4096]{1,0:T(8,128)(2,1)}), bf16[256,1024]{1,0:T(8,128)(2,1)}) %reduce-scatter.2.cloned.1.call-update) | async-done | bytes 524304 | tf_op jit(solution)/shard_map/reduce_scatter | solution.py:93
  (9 shorter events, 0.1 us)
Async XLA Ops:
  6.5 86.4 %reduce-scatter.2.cloned.1.call-start = ((), (), s32[]{:S(2)}) async-start(), calls=%async_computation.1 | async-start | bytes 2621440 | tf_op jit(solution)/shard_map/reduce_scatter | solution.py:93
  7.4 37.6 %collective-permute-start = (bf16[2,256,128]{2,1,0:T(8,128)(2,1)S(1)}, bf16[2,256,128]{2,1,0:T(8,128)(2,1)S(1)}, u32[]{:S(2)}, u32[]{:S(2)}) collective-permute-start(bf16[2,256,128]{2,1,0:T(8,128)(2,1)S(1)} %pad_maximum_fusion), channel_id=1, source_target_pairs={{0,4},{4,8},{8,12},{1,5},{5,9},{9,13},{2,6},{6,10},{10,14},{3,7},{... | collective-permute-start | bytes 393224 | tf_op jit(solution)/shard_map/ppermute | solution.py:13
  45.0 2.8 %copy-start = (bf16[256,128]{1,0:T(8,128)(2,1)S(1)}, bf16[256,128]{1,0:T(8,128)(2,1)}, u32[]{:S(2)}) copy-start(bf16[256,128]{1,0:T(8,128)(2,1)} %param.11) | copy-start | bytes 196612
Sparse Core Ops, SparseCore 0:
  63.1 29.7 reduce-scatter.1
where the time goes:
time: 100 us; the launch traced here: 99.8 us
  waiting for transfers between devices  29.9 us (30%)
  blocking collectives  29.3 us (29%)
  matrix products  15.1 us (15%)
  between operations  13.5 us (14%)
  other arithmetic  5.03 us (5%)
  starting transfers between devices  4.94 us (5%)
  local copies, waits for them, and re-layouts  1.87 us (2%)
    reduce_scatter x1, waiting for transfers between devices, local(): lax.psum_scatter(partial_value.astype(jnp.bfloat16), 'tp', scatter_dimens...  29.9 us
    all_gather x1, blocking collectives, local(): piece_k = lax.all_gather(prompt_keys, 'ctx', axis=0, tiled=True)  15 us
    all_gather x1, blocking collectives, local(): piece_v = lax.all_gather(prompt_values, 'ctx', axis=0, tiled=True)  14.4 us
    dot_general x1, matrix products, local(): jnp.dot(attended, out_weight, preferred_element_type=jnp.float32)  7.11 us
    ppermute x1, starting transfers between devices, shifted(): return lax.ppermute(block, axis, route)  4.94 us
    dot_general x3, matrix products, block_stats(): jnp.einsum('kgrs,skd->kgrd', weights.astype(jnp.bfloat16), values, prefer...  4.63 us
    dot_general x3, matrix products, block_stats(): jnp.einsum('rkgd,skd->kgrs', query_rows, keys, preferred_element_type=jnp...  3.31 us
    reduce_sum x3, other arithmetic, block_stats(): total = jnp.sum(weights, axis=-1)  2.26 us
  transfers between devices with their start and end apart: 2, of which 1 were waited for; matrix products, arithmetic and copies ran while one was open for 3% of the time, Pallas kernels for 0%

commit v1 on v0

v1 whole, which is shorter than its diff:
```python
import functools

import jax
import jax.numpy as jnp
from jax import lax
from jax.experimental import pallas as pl
from jax.experimental.pallas import tpu as pltpu
from jax.sharding import PartitionSpec as P

HD = 128
SUB = 256
MESH = pl.DeviceIdType.MESH
SCALE = 1.4426950408889634 / HD**0.5
MASKED = -1e30


def kernel(
    n,
    n_tp,
    q_hbm,
    rk_hbm,
    rv_hbm,
    pk_hbm,
    pv_hbm,
    lengths,
    w_hbm,
    out_hbm,
    q,
    w,
    key_all,
    value_all,
    resp_k,
    resp_v,
    bias,
    acc,
    tops,
    att,
    send1,
    recv1,
    send2,
    recv2,
    near,
    out,
    in_sem,
    w_sem,
    out_sem,
    gather_send,
    gather_recv,
    resp_send,
    resp_recv,
    send1_sem,
    recv1_sem,
    send2_sem,
    recv2_sem,
):
    me = lax.axis_index("ctx")
    t = lax.axis_index("tp")
    rows = q.shape[0]
    heads = q.shape[1] // HD
    width = out.shape[1]
    subs = width // SUB
    low = lax.rem(t, 2)
    high = t // 2
    sibling = high * 2 + 1 - low
    across = lax.rem(t + n_tp // 2, n_tp)
    has_left = me > 0
    has_right = me < n - 1

    local_in = [
        pltpu.make_async_copy(q_hbm, q, in_sem.at[0]),
        pltpu.make_async_copy(pk_hbm, key_all.at[me], in_sem.at[1]),
        pltpu.make_async_copy(pv_hbm, value_all.at[me], in_sem.at[2]),
        pltpu.make_async_copy(rk_hbm, resp_k.at[1], in_sem.at[3]),
        pltpu.make_async_copy(rv_hbm, resp_v.at[1], in_sem.at[4]),
    ]
    for copy in local_in:
        copy.start()

    barrier = pltpu.get_barrier_semaphore()

    @pl.when(has_left)
    def _():
        pl.semaphore_signal(barrier, inc=1, device_id={"ctx": me - 1}, device_id_type=MESH)

    @pl.when(has_right)
    def _():
        pl.semaphore_signal(barrier, inc=1, device_id={"ctx": me + 1}, device_id_type=MESH)

    for partner in (sibling, across):
        pl.semaphore_signal(barrier, inc=1, device_id={"tp": partner}, device_id_type=MESH)
    peers = 2 + has_left.astype(jnp.int32) + has_right.astype(jnp.int32)
    pl.semaphore_wait(barrier, peers)

    def prompt_copy(which, chunk, src, direction, slot):
        dst = (key_all, value_all)[which].at[chunk]
        return pltpu.make_async_remote_copy(
            src_ref=src,
            dst_ref=dst,
            send_sem=gather_send.at[which, slot],
            recv_sem=gather_recv.at[which, chunk],
            device_id={"ctx": me + direction},
            device_id_type=MESH,
        )

    def response_copy(which):
        return pltpu.make_async_remote_copy(
            src_ref=(rk_hbm, rv_hbm)[which],
            dst_ref=(resp_k, resp_v)[which].at[0],
            send_sem=resp_send.at[which],
            recv_sem=resp_recv.at[which],
            device_id={"ctx": me + 1},
            device_id_type=MESH,
        )

    @pl.when(has_right)
    def _():
        prompt_copy(0, me, pk_hbm, 1, n).start()
        prompt_copy(1, me, pv_hbm, 1, n).start()
        response_copy(0).start()
        response_copy(1).start()

    @pl.when(has_left)
    def _():
        prompt_copy(0, me, pk_hbm, -1, n + 1).start()
        prompt_copy(1, me, pv_hbm, -1, n + 1).start()

    w_copy = pltpu.make_async_copy(w_hbm, w, w_sem)
    w_copy.start()

    base = me * rows
    row_pos = base + lax.broadcasted_iota(jnp.int32, (rows, rows), 0)
    key_pos = base + lax.broadcasted_iota(jnp.int32, (rows, rows), 1)
    first = jnp.zeros((rows, rows), jnp.int32)
    start = jnp.int32(0)
    for r in range(lengths.shape[0]):
        first = jnp.where(row_pos >= start, start, first)
        start = start + lengths[r]
    own = (key_pos >= first) & (key_pos <= row_pos)
    bias[1] = jnp.where(own, 0.0, MASKED)
    bias[0] = jnp.where(key_pos - rows >= first, 0.0, MASKED)

    for copy in local_in:
        copy.wait()

    def extended(values):
        return jnp.concatenate([values, jnp.ones(values.shape, values.dtype)], axis=1)

    def attend(parts, fresh):
        for h in range(heads):
            query = q[:, h * HD : (h + 1) * HD]
            scores = []
            for keys, _, extra in parts:
                s = lax.dot_general(
                    query, keys[...], (((1,), (1,)), ((), ())), preferred_element_type=jnp.float32
                )
                s = s * SCALE
                if extra is not None:
                    s = s + extra[...]
                scores.append(s)
            top = functools.reduce(
                jnp.maximum, [jnp.max(s, axis=1, keepdims=True) for s in scores]
            )
            if not fresh:
                before = tops[h]
                top = jnp.maximum(top, before)
            added = None
            for s, (_, values, _) in zip(scores, parts):
                p = jnp.exp2(s - top).astype(jnp.bfloat16)
                term = jnp.dot(p, extended(values[...]), preferred_element_type=jnp.float32)
                added = term if added is None else added + term
            if fresh:
                acc[h] = added
            else:
                acc[h] = acc[h] * jnp.exp2(before - top) + added
            tops[h] = top

    attend(
        [(key_all.at[me], value_all.at[me], None), (resp_k.at[1], resp_v.at[1], bias.at[1])], True
    )

    @pl.when(has_left)
    def _():
        for which in range(2):
            response_copy(which).wait_recv()

    @pl.when(me == 0)
    def _():
        resp_k[0] = jnp.zeros_like(resp_k[0])
        resp_v[0] = jnp.zeros_like(resp_v[0])

    left_count = me
    right_count = n - 1 - me
    both = jnp.minimum(left_count, right_count)

    def arrival(j):
        s = (j + 1) // 2
        paired = jnp.where(lax.rem(j, 2) == 1, -s, s)
        single = jnp.where(left_count > right_count, both - j, j - both)
        return me + jnp.where(j <= 2 * both, paired, single)

    def take(j):
        chunk = arrival(j)
        for which in range(2):
            ref = (key_all, value_all)[which].at[chunk]
            prompt_copy(which, chunk, ref, 1, chunk).wait_recv()

            @pl.when((chunk < me) & has_right)
            def _():
                prompt_copy(which, chunk, ref, 1, chunk).start()

            @pl.when((chunk > me) & has_left)
            def _():
                prompt_copy(which, chunk, ref, -1, chunk).start()

        return chunk

    chunk = take(jnp.int32(1))
    attend(
        [
            (key_all.at[chunk], value_all.at[chunk], None),
            (resp_k.at[0], resp_v.at[0], bias.at[0]),
        ],
        False,
    )

    def later(j, carry):
        chunk = take(j)
        attend([(key_all.at[chunk], value_all.at[chunk], None)], False)
        return carry

    lax.fori_loop(2, n, later, 0)

    for h in range(heads):
        att[:, h * HD : (h + 1) * HD] = (acc[h, :, :HD] / acc[h, :, HD:]).astype(jnp.bfloat16)

    w_copy.wait()

    def product(block, sub):
        columns = pl.ds(pl.multiple_of(block * width + sub * SUB, SUB), SUB)
        return jnp.dot(att[...], w[:, columns], preferred_element_type=jnp.float32)

    def to_sibling(half, sub):
        return pltpu.make_async_remote_copy(
            src_ref=send1.at[half, sub],
            dst_ref=recv1.at[half, sub],
            send_sem=send1_sem.at[half, sub],
            recv_sem=recv1_sem.at[half, sub],
            device_id={"tp": sibling},
            device_id_type=MESH,
        )

    def to_across(sub):
        return pltpu.make_async_remote_copy(
            src_ref=send2.at[sub],
            dst_ref=recv2.at[sub],
            send_sem=send2_sem.at[sub],
            recv_sem=recv2_sem.at[sub],
            device_id={"tp": across},
            device_id_type=MESH,
        )

    def hand_sibling(half, side, sub):
        send1[half, sub] = product(side * 2 + 1 - low, sub).astype(jnp.bfloat16)
        to_sibling(half, sub).start()

    hand_sibling(0, 1 - high, 0)
    for sub in range(subs):
        if sub + 1 < subs:
            hand_sibling(0, 1 - high, sub + 1)
        mine = product((1 - high) * 2 + low, sub)
        to_sibling(0, sub).wait_recv()
        send2[sub] = (mine + recv1[0, sub].astype(jnp.float32)).astype(jnp.bfloat16)
        to_across(sub).start()
    for sub in range(subs):
        hand_sibling(1, high, sub)
    for sub in range(subs):
        near[sub] = product(high * 2 + low, sub)
    for sub in range(subs):
        to_sibling(1, sub).wait_recv()
        near[sub] = near[sub] + recv1[1, sub].astype(jnp.float32)

    def out_copy(sub):
        columns = pl.ds(sub * SUB, SUB)
        return pltpu.make_async_copy(out.at[:, columns], out_hbm.at[:, columns], out_sem.at[sub])

    for sub in range(subs):
        to_across(sub).wait_recv()
        out[:, sub * SUB : (sub + 1) * SUB] = (
            near[sub] + recv2[sub].astype(jnp.float32)
        ).astype(jnp.bfloat16)
        out_copy(sub).start()

    for sub in range(subs):
        to_sibling(0, sub).wait_send()
        to_sibling(1, sub).wait_send()
        to_across(sub).wait_send()

    @pl.when(has_right)
    def _():
        for which in range(2):
            prompt_copy(which, me, key_all.at[me], 1, n).wait_send()
            response_copy(which).wait_send()

    @pl.when(has_left)
    def _():
        for which in range(2):
            prompt_copy(which, me, key_all.at[me], -1, n + 1).wait_send()

    def drain(j, carry):
        chunk = arrival(j)

        @pl.when(((chunk < me) & has_right) | ((chunk > me) & has_left))
        def _():
            for which in range(2):
                prompt_copy(which, chunk, key_all.at[chunk], 1, chunk).wait_send()

        return carry

    lax.fori_loop(1, n, drain, 0)
    for sub in range(subs):
        out_copy(sub).wait()


def local(mesh_shape, queries, rk, rv, pk, pv, lengths, out_weight):
    n, n_tp = mesh_shape["ctx"], mesh_shape["tp"]
    rows, query_cols = queries.shape
    depth, out_cols = out_weight.shape
    width = out_cols // n_tp
    subs = width // SUB
    heads = query_cols // HD
    assert rk.shape[1] == HD and n_tp == 4
    bf16, f32 = jnp.bfloat16, jnp.float32
    dma = pltpu.SemaphoreType.DMA
    any_space = pl.BlockSpec(memory_space=pl.ANY)
    return pl.pallas_call(
        functools.partial(kernel, n, n_tp),
        out_shape=jax.ShapeDtypeStruct((rows, width), bf16),
        in_specs=[any_space] * 5 + [pl.BlockSpec(memory_space=pltpu.SMEM), any_space],
        out_specs=any_space,
        scratch_shapes=[
            pltpu.VMEM((rows, query_cols), bf16),
            pltpu.VMEM((depth, out_cols), bf16),
            pltpu.VMEM((n, rows, HD), bf16),
            pltpu.VMEM((n, rows, HD), bf16),
            pltpu.VMEM((2, rows, HD), bf16),
            pltpu.VMEM((2, rows, HD), bf16),
            pltpu.VMEM((2, rows, rows), f32),
            pltpu.VMEM((heads, rows, 2 * HD), f32),
            pltpu.VMEM((heads, rows, 1), f32),
            pltpu.VMEM((rows, query_cols), bf16),
            pltpu.VMEM((2, subs, rows, SUB), bf16),
            pltpu.VMEM((2, subs, rows, SUB), bf16),
            pltpu.VMEM((subs, rows, SUB), bf16),
            pltpu.VMEM((subs, rows, SUB), bf16),
            pltpu.VMEM((subs, rows, SUB), f32),
            pltpu.VMEM((rows, width), bf16),
            dma((5,)),
            dma,
            dma((subs,)),
            dma((2, n + 2)),
            dma((2, n)),
            dma((2,)),
            dma((2,)),
            dma((2, subs)),
            dma((2, subs)),
            dma((subs,)),
            dma((subs,)),
        ],
        compiler_params=pltpu.CompilerParams(
            collective_id=0, has_side_effects=True, vmem_limit_bytes=48 * 1024 * 1024
        ),
    )(queries, rk, rv, pk, pv, lengths, out_weight)


def solution(mesh):
    placed = (
        P(("groups", "ctx"), "tp"),
        P(("groups", "ctx"), "tp"),
        P(("groups", "ctx"), "tp"),
        P(("groups", "ctx"), "tp"),
        P(("groups", "ctx"), "tp"),
        P("groups"),
        P("tp", None),
    )
    return jax.shard_map(
        functools.partial(local, dict(mesh.shape)),
        mesh=mesh,
        in_specs=placed,
        out_specs=P(("groups", "ctx"), "tp"),
        check_vma=False,
    )
```

time: 100 us -> 48 us (0.48)
  Pallas kernels: 0 us -> 41.8 us
  waiting for transfers between devices: 29.9 us -> 0 us
  blocking collectives: 29.3 us -> 0 us
  matrix products: 15.1 us -> 0 us
  between operations: 13.5 us -> 0.02 us
  other arithmetic: 5.03 us -> 0 us
  starting transfers between devices: 4.94 us -> 0 us
  local copies, waits for them, and re-layouts: 1.87 us -> 5.85 us
    pallas_call x0 -> x1, Pallas kernels: none -> 41.8 us  [local(): pl.pallas_call(functools.partial(kernel, n, n_tp), out_shape=jax.ShapeDty...]
    reduce_scatter x1 -> x0, waiting for transfers between devices: 29.9 us -> none  [local(): lax.psum_scatter(partial_value.astype(jnp.bfloat16), 'tp', scatter_dimens...]
    all_gather x2 -> x0, blocking collectives: 29.3 us -> none  [the longest x1 15 us: local(): piece_k = lax.all_gather(prompt_keys, 'ctx', axis=0, tiled=True)]
    dot_general x7 -> x0, matrix products: 15.1 us -> none  [the longest x1 7.11 us: local(): jnp.dot(attended, out_weight, preferred_element_type=jnp.float32)]
    ppermute x1 -> x0, starting transfers between devices: 4.94 us -> none  [shifted(): return lax.ppermute(block, axis, route)]
    unnamed x3 -> x13, local copies, waits for them, and re-layouts: 1.25 us -> 5.85 us
    reduce_sum x3 -> x0, other arithmetic: 2.26 us -> none  [block_stats(): total = jnp.sum(weights, axis=-1)]
    another operation x2 -> x0, other arithmetic: 1.71 us -> none  [the longest x1 0.88 us: local(): previous = shifted(jnp.stack([response_keys, response_values]), 'ctx', 1)]
  transfers between devices with their start and end apart: 2 -> 0, of which waited for: 1 -> 0; matrix products, arithmetic and copies ran while one was open for 3% -> 0% of each run, Pallas kernels for 0% -> 0%
where the time goes in v1:
time: 48 us; the launch traced here: 47.6 us
  Pallas kernels  41.8 us (87%)
  local copies, waits for them, and re-layouts  5.85 us (12%)
    pallas_call x1, Pallas kernels, local(): pl.pallas_call(functools.partial(kernel, n, n_tp), out_shape=jax.ShapeDty...  41.8 us
    unnamed x13, local copies, waits for them, and re-layouts  5.85 us

profile of v1, /device:TPU:0, one launch (start us, length us, event | category | flops | bytes accessed | tf_op | source)
XLA Modules:
  0.0 47.6 jit_solution(9739659202636882977)
XLA Ops:
  0.0 0.0 copy-start
  0.0 1.0 %copy-done = bf16[256,1024]{1,0:T(8,128)(2,1)S(1)} copy-done((bf16[256,1024]{1,0:T(8,128)(2,1)S(1)}, bf16[256,1024]{1,0:T(8,128)(2,1)}, u32[]{:S(2)}) %copy-start) | copy-done | bytes 524312
  1.0 0.0 copy-start.1
  1.0 0.8 %copy-done.1 = bf16[256,128]{1,0:T(8,128)(2,1)S(1)} copy-done((bf16[256,128]{1,0:T(8,128)(2,1)S(1)}, bf16[256,128]{1,0:T(8,128)(2,1)}, u32[]{:S(2)}) %copy-start.1) | copy-done | bytes 65560
  1.9 0.0 copy-start.2
  1.9 0.8 %copy-done.2 = bf16[256,128]{1,0:T(8,128)(2,1)S(1)} copy-done((bf16[256,128]{1,0:T(8,128)(2,1)S(1)}, bf16[256,128]{1,0:T(8,128)(2,1)}, u32[]{:S(2)}) %copy-start.2) | copy-done | bytes 65560
  2.7 0.0 copy-start.3
  2.7 0.8 %copy-done.3 = bf16[256,128]{1,0:T(8,128)(2,1)S(1)} copy-done((bf16[256,128]{1,0:T(8,128)(2,1)S(1)}, bf16[256,128]{1,0:T(8,128)(2,1)}, u32[]{:S(2)}) %copy-start.3) | copy-done | bytes 65560
  3.6 0.0 copy-start.4
  3.6 0.8 %copy-done.4 = bf16[256,128]{1,0:T(8,128)(2,1)S(1)} copy-done((bf16[256,128]{1,0:T(8,128)(2,1)S(1)}, bf16[256,128]{1,0:T(8,128)(2,1)}, u32[]{:S(2)}) %copy-start.4) | copy-done | bytes 65560
  4.4 0.0 copy-start.5
  4.4 0.7 %copy-done.5 = s32[6]{0:T(128)S(1)} copy-done((s32[6]{0:T(128)S(1)}, s32[6]{0:T(128)}, u32[]{:S(2)}) %copy-start.5) | copy-done | bytes 48
  5.1 41.8 %shard_map.73 = bf16[256,1024]{1,0:T(8,128)(2,1)S(1)} custom-call(bf16[256,1024]{1,0:T(8,128)(2,1)S(1)} %copy-done, bf16[256,128]{1,0:T(8,128)(2,1)S(1)} %copy-done.1, bf16[256,128]{1,0:T(8,128)(2,1)S(1)} %copy-done.2, bf16[256,128]{1,0:T(8,128)(2,1)S(1)} %copy-done.3, bf16[256,128]{1,0:T(8,128)(2,1)S(1)} %copy-done.4, s32[6]{0:T(128)S(1)} %copy-done.5, ...), custom_call_target="tpu_custom_call" | custom-call | tf_op jit(solution)/shard_map/pallas_call | solution.py:335
  46.8 0.8 %copy.9 = bf16[256,1024]{1,0:T(8,128)(2,1)} copy(bf16[256,1024]{1,0:T(8,128)(2,1)S(1)} %shard_map.73) | data formatting | bytes 1048576
Async XLA Ops:
  0.0 1.0 %copy-start = (bf16[256,1024]{1,0:T(8,128)(2,1)S(1)}, bf16[256,1024]{1,0:T(8,128)(2,1)}, u32[]{:S(2)}) copy-start(bf16[256,1024]{1,0:T(8,128)(2,1)} %q_hbm.1) | copy-start | bytes 1572868
  1.0 0.8 %copy-start.1 = (bf16[256,128]{1,0:T(8,128)(2,1)S(1)}, bf16[256,128]{1,0:T(8,128)(2,1)}, u32[]{:S(2)}) copy-start(bf16[256,128]{1,0:T(8,128)(2,1)} %rk_hbm.1) | copy-start | bytes 196612
  1.9 0.8 %copy-start.2 = (bf16[256,128]{1,0:T(8,128)(2,1)S(1)}, bf16[256,128]{1,0:T(8,128)(2,1)}, u32[]{:S(2)}) copy-start(bf16[256,128]{1,0:T(8,128)(2,1)} %rv_hbm.1) | copy-start | bytes 196612
  2.7 0.8 %copy-start.3 = (bf16[256,128]{1,0:T(8,128)(2,1)S(1)}, bf16[256,128]{1,0:T(8,128)(2,1)}, u32[]{:S(2)}) copy-start(bf16[256,128]{1,0:T(8,128)(2,1)} %pk_hbm.1) | copy-start | bytes 196612
  3.6 0.8 %copy-start.4 = (bf16[256,128]{1,0:T(8,128)(2,1)S(1)}, bf16[256,128]{1,0:T(8,128)(2,1)}, u32[]{:S(2)}) copy-start(bf16[256,128]{1,0:T(8,128)(2,1)} %pv_hbm.1) | copy-start | bytes 196612
  4.4 0.7 %copy-start.5 = (s32[6]{0:T(128)S(1)}, s32[6]{0:T(128)}, u32[]{:S(2)}) copy-start(s32[6]{0:T(128)} %lengths.1) | copy-start | bytes 76

commit v2 on v1

--- a/solution.py
+++ b/solution.py
@@ -12,6 +12,7 @@
 MESH = pl.DeviceIdType.MESH
 SCALE = 1.4426950408889634 / HD**0.5
 MASKED = -1e30
+VMEM_BYTES = 63 * 1024 * 1024
 
 
 def kernel(
@@ -22,9 +23,10 @@
     rv_hbm,
     pk_hbm,
     pv_hbm,
-    lengths,
+    lengths_hbm,
     w_hbm,
     out_hbm,
+    lengths,
     q,
     w,
     key_all,
@@ -72,9 +74,13 @@
         pltpu.make_async_copy(pv_hbm, value_all.at[me], in_sem.at[2]),
         pltpu.make_async_copy(rk_hbm, resp_k.at[1], in_sem.at[3]),
         pltpu.make_async_copy(rv_hbm, resp_v.at[1], in_sem.at[4]),
+        pltpu.make_async_copy(lengths_hbm, lengths, in_sem.at[5]),
     ]
     for copy in local_in:
         copy.start()
+
+    w_copy = pltpu.make_async_copy(w_hbm, w, w_sem)
+    w_copy.start()
 
     barrier = pltpu.get_barrier_semaphore()
 
@@ -116,16 +122,14 @@
     def _():
         prompt_copy(0, me, pk_hbm, 1, n).start()
         prompt_copy(1, me, pv_hbm, 1, n).start()
-        response_copy(0).start()
-        response_copy(1).start()
 
     @pl.when(has_left)
     def _():
         prompt_copy(0, me, pk_hbm, -1, n + 1).start()
         prompt_copy(1, me, pv_hbm, -1, n + 1).start()
 
-    w_copy = pltpu.make_async_copy(w_hbm, w, w_sem)
-    w_copy.start()
+    for copy in local_in:
+        copy.wait()
 
     base = me * rows
     row_pos = base + lax.broadcasted_iota(jnp.int32, (rows, rows), 0)
@@ -138,9 +142,6 @@
     own = (key_pos >= first) & (key_pos <= row_pos)
     bias[1] = jnp.where(own, 0.0, MASKED)
     bias[0] = jnp.where(key_pos - rows >= first, 0.0, MASKED)
-
-    for copy in local_in:
-        copy.wait()
 
     def extended(values):
         return jnp.concatenate([values, jnp.ones(values.shape, values.dtype)], axis=1)
@@ -178,57 +179,46 @@
         [(key_all.at[me], value_all.at[me], None), (resp_k.at[1], resp_v.at[1], bias.at[1])], True
     )
 
-    @pl.when(has_left)
-    def _():
-        for which in range(2):
-            response_copy(which).wait_recv()
-
-    @pl.when(me == 0)
-    def _():
-        resp_k[0] = jnp.zeros_like(resp_k[0])
-        resp_v[0] = jnp.zeros_like(resp_v[0])
-
-    left_count = me
-    right_count = n - 1 - me
-    both = jnp.minimum(left_count, right_count)
-
-    def arrival(j):
-        s = (j + 1) // 2
-        paired = jnp.where(lax.rem(j, 2) == 1, -s, s)
-        single = jnp.where(left_count > right_count, both - j, j - both)
-        return me + jnp.where(j <= 2 * both, paired, single)
-
-    def take(j):
-        chunk = arrival(j)
+    @pl.when(has_right)
+    def _():
+        response_copy(0).start()
+        response_copy(1).start()
+
+    def hand_on(chunk, direction, onward):
         for which in range(2):
             ref = (key_all, value_all)[which].at[chunk]
-            prompt_copy(which, chunk, ref, 1, chunk).wait_recv()
-
-            @pl.when((chunk < me) & has_right)
-            def _():
-                prompt_copy(which, chunk, ref, 1, chunk).start()
-
-            @pl.when((chunk > me) & has_left)
-            def _():
-                prompt_copy(which, chunk, ref, -1, chunk).start()
-
-        return chunk
-
-    chunk = take(jnp.int32(1))
-    attend(
-        [
-            (key_all.at[chunk], value_all.at[chunk], None),
-            (resp_k.at[0], resp_v.at[0], bias.at[0]),
-        ],
-        False,
-    )
-
-    def later(j, carry):
-        chunk = take(j)
-        attend([(key_all.at[chunk], value_all.at[chunk], None)], False)
+            copy = prompt_copy(which, chunk, ref, direction, chunk)
+            copy.wait_recv()
+            pl.when(onward)(copy.start)
+
+    def ring(s, carry):
+        from_left, from_right = me - s, me + s
+
+        @pl.when(from_left >= 0)
+        def _():
+            hand_on(from_left, 1, has_right)
+
+        @pl.when(from_right < n)
+        def _():
+            hand_on(from_right, -1, has_left)
+
+        @pl.when(from_left >= 0)
+        def _():
+            attend([(key_all.at[from_left], value_all.at[from_left], None)], False)
+
+        @pl.when(from_right < n)
+        def _():
+            attend([(key_all.at[from_right], value_all.at[from_right], None)], False)
+
+        @pl.when(has_left & (s == jnp.where(has_right, 2, 1)))
+        def _():
+            for which in range(2):
+                response_copy(which).wait_recv()
+            attend([(resp_k.at[0], resp_v.at[0], bias.at[0])], False)
+
         return carry
 
-    lax.fori_loop(2, n, later, 0)
+    lax.fori_loop(1, n, ring, 0)
 
     for h in range(heads):
         att[:, h * HD : (h + 1) * HD] = (acc[h, :, :HD] / acc[h, :, HD:]).astype(jnp.bfloat16)
@@ -306,9 +296,7 @@
         for which in range(2):
             prompt_copy(which, me, key_all.at[me], -1, n + 1).wait_send()
 
-    def drain(j, carry):
-        chunk = arrival(j)
-
+    def drain(chunk, carry):
         @pl.when(((chunk < me) & has_right) | ((chunk > me) & has_left))
         def _():
             for which in range(2):
@@ -316,7 +304,7 @@
 
         return carry
 
-    lax.fori_loop(1, n, drain, 0)
+    lax.fori_loop(0, n, drain, 0)
     for sub in range(subs):
         out_copy(sub).wait()
 
@@ -331,13 +319,14 @@
     assert rk.shape[1] == HD and n_tp == 4
     bf16, f32 = jnp.bfloat16, jnp.float32
     dma = pltpu.SemaphoreType.DMA
-    any_space = pl.BlockSpec(memory_space=pl.ANY)
+    in_hbm = pl.BlockSpec(memory_space=pltpu.HBM)
     return pl.pallas_call(
         functools.partial(kernel, n, n_tp),
         out_shape=jax.ShapeDtypeStruct((rows, width), bf16),
-        in_specs=[any_space] * 5 + [pl.BlockSpec(memory_space=pltpu.SMEM), any_space],
-        out_specs=any_space,
+        in_specs=[in_hbm] * 7,
+        out_specs=in_hbm,
         scratch_shapes=[
+            pltpu.SMEM(lengths.shape, jnp.int32),
             pltpu.VMEM((rows, query_cols), bf16),
             pltpu.VMEM((depth, out_cols), bf16),
             pltpu.VMEM((n, rows, HD), bf16),
@@ -354,7 +343,7 @@
             pltpu.VMEM((subs, rows, SUB), bf16),
             pltpu.VMEM((subs, rows, SUB), f32),
             pltpu.VMEM((rows, width), bf16),
-            dma((5,)),
+            dma((6,)),
             dma,
             dma((subs,)),
             dma((2, n + 2)),
@@ -367,7 +356,7 @@
             dma((subs,)),
         ],
         compiler_params=pltpu.CompilerParams(
-            collective_id=0, has_side_effects=True, vmem_limit_bytes=48 * 1024 * 1024
+            collective_id=0, has_side_effects=True, vmem_limit_bytes=VMEM_BYTES
         ),
     )(queries, rk, rv, pk, pv, lengths, out_weight)
 

time: 48 us -> 38.8 us (0.81)
  Pallas kernels: 41.8 us -> 36.7 us
  local copies, waits for them, and re-layouts: 5.85 us -> 1.87 us
    pallas_call x1, Pallas kernels: 41.8 us -> 36.7 us  [local(): pl.pallas_call(functools.partial(kernel, n, n_tp), out_shape=jax.ShapeDty...]
    unnamed x13 -> x1, local copies, waits for them, and re-layouts: 5.85 us -> 1.87 us
where the time goes in v2:
time: 38.8 us; the launch traced here: 38.6 us
  Pallas kernels  36.7 us (95%)
  local copies, waits for them, and re-layouts  1.87 us (5%)
    pallas_call x1, Pallas kernels, local(): pl.pallas_call(functools.partial(kernel, n, n_tp), out_shape=jax.ShapeDty...  36.7 us
    unnamed x1, local copies, waits for them, and re-layouts  1.87 us

profile of v2, /device:TPU:0, one launch (start us, length us, event | category | flops | bytes accessed | tf_op | source)
XLA Modules:
  0.0 38.6 jit_solution(3822289916199100099)
XLA Ops:
  0.0 36.7 %shard_map.73 = bf16[256,1024]{1,0:T(8,128)(2,1)} custom-call(bf16[256,1024]{1,0:T(8,128)(2,1)} %q_hbm.1, bf16[256,128]{1,0:T(8,128)(2,1)} %rk_hbm.1, bf16[256,128]{1,0:T(8,128)(2,1)} %rv_hbm.1, bf16[256,128]{1,0:T(8,128)(2,1)} %pk_hbm.1, bf16[256,128]{1,0:T(8,128)(2,1)} %pv_hbm.1, s32[6]{0:T(128)} %lengths_hbm.1, bf16[1024,4096]{1,0:T(8,128)(2,1)} %w_hbm.1), custom_call_target="tpu_custom_call" | custom-call | tf_op jit(solution)/shard_map/pallas_call | solution.py:323
  36.8 1.9 %copy.9 = bf16[256,1024]{1,0:T(8,128)(2,1)} copy(bf16[256,1024]{1,0:T(8,128)(2,1)} %shard_map.73) | data formatting | bytes 1048576

commit v3 on v2

--- a/solution.py
+++ b/solution.py
@@ -12,7 +12,7 @@
 MESH = pl.DeviceIdType.MESH
 SCALE = 1.4426950408889634 / HD**0.5
 MASKED = -1e30
-VMEM_BYTES = 63 * 1024 * 1024
+VMEM_BYTES = 62 * 1024 * 1024
 
 
 def kernel(
@@ -25,7 +25,7 @@
     pv_hbm,
     lengths_hbm,
     w_hbm,
-    out_hbm,
+    out,
     lengths,
     q,
     w,
@@ -42,10 +42,8 @@
     send2,
     recv2,
     near,
-    out,
     in_sem,
     w_sem,
-    out_sem,
     gather_send,
     gather_recv,
     resp_send,
@@ -95,39 +93,6 @@
     for partner in (sibling, across):
         pl.semaphore_signal(barrier, inc=1, device_id={"tp": partner}, device_id_type=MESH)
     peers = 2 + has_left.astype(jnp.int32) + has_right.astype(jnp.int32)
-    pl.semaphore_wait(barrier, peers)
-
-    def prompt_copy(which, chunk, src, direction, slot):
-        dst = (key_all, value_all)[which].at[chunk]
-        return pltpu.make_async_remote_copy(
-            src_ref=src,
-            dst_ref=dst,
-            send_sem=gather_send.at[which, slot],
-            recv_sem=gather_recv.at[which, chunk],
-            device_id={"ctx": me + direction},
-            device_id_type=MESH,
-        )
-
-    def response_copy(which):
-        return pltpu.make_async_remote_copy(
-            src_ref=(rk_hbm, rv_hbm)[which],
-            dst_ref=(resp_k, resp_v)[which].at[0],
-            send_sem=resp_send.at[which],
-            recv_sem=resp_recv.at[which],
-            device_id={"ctx": me + 1},
-            device_id_type=MESH,
-        )
-
-    @pl.when(has_right)
-    def _():
-        prompt_copy(0, me, pk_hbm, 1, n).start()
-        prompt_copy(1, me, pv_hbm, 1, n).start()
-
-    @pl.when(has_left)
-    def _():
-        prompt_copy(0, me, pk_hbm, -1, n + 1).start()
-        prompt_copy(1, me, pv_hbm, -1, n + 1).start()
-
     for copy in local_in:
         copy.wait()
 
@@ -142,6 +107,39 @@
     own = (key_pos >= first) & (key_pos <= row_pos)
     bias[1] = jnp.where(own, 0.0, MASKED)
     bias[0] = jnp.where(key_pos - rows >= first, 0.0, MASKED)
+
+    pl.semaphore_wait(barrier, peers)
+
+    def prompt_copy(which, chunk, src, direction, slot):
+        dst = (key_all, value_all)[which].at[chunk]
+        return pltpu.make_async_remote_copy(
+            src_ref=src,
+            dst_ref=dst,
+            send_sem=gather_send.at[which, slot],
+            recv_sem=gather_recv.at[which, chunk],
+            device_id={"ctx": me + direction},
+            device_id_type=MESH,
+        )
+
+    def response_copy(which):
+        return pltpu.make_async_remote_copy(
+            src_ref=(rk_hbm, rv_hbm)[which],
+            dst_ref=(resp_k, resp_v)[which].at[0],
+            send_sem=resp_send.at[which],
+            recv_sem=resp_recv.at[which],
+            device_id={"ctx": me + 1},
+            device_id_type=MESH,
+        )
+
+    @pl.when(has_right)
+    def _():
+        prompt_copy(0, me, pk_hbm, 1, n).start()
+        prompt_copy(1, me, pv_hbm, 1, n).start()
+
+    @pl.when(has_left)
+    def _():
+        prompt_copy(0, me, pk_hbm, -1, n + 1).start()
+        prompt_copy(1, me, pv_hbm, -1, n + 1).start()
 
     def extended(values):
         return jnp.concatenate([values, jnp.ones(values.shape, values.dtype)], axis=1)
@@ -269,16 +267,11 @@
         to_sibling(1, sub).wait_recv()
         near[sub] = near[sub] + recv1[1, sub].astype(jnp.float32)
 
-    def out_copy(sub):
-        columns = pl.ds(sub * SUB, SUB)
-        return pltpu.make_async_copy(out.at[:, columns], out_hbm.at[:, columns], out_sem.at[sub])
-
     for sub in range(subs):
         to_across(sub).wait_recv()
         out[:, sub * SUB : (sub + 1) * SUB] = (
             near[sub] + recv2[sub].astype(jnp.float32)
         ).astype(jnp.bfloat16)
-        out_copy(sub).start()
 
     for sub in range(subs):
         to_sibling(0, sub).wait_send()
@@ -305,8 +298,6 @@
         return carry
 
     lax.fori_loop(0, n, drain, 0)
-    for sub in range(subs):
-        out_copy(sub).wait()
 
 
 def local(mesh_shape, queries, rk, rv, pk, pv, lengths, out_weight):
@@ -322,9 +313,9 @@
     in_hbm = pl.BlockSpec(memory_space=pltpu.HBM)
     return pl.pallas_call(
         functools.partial(kernel, n, n_tp),
-        out_shape=jax.ShapeDtypeStruct((rows, width), bf16),
+        out_shape=pltpu.VMEM((rows, width), bf16),
         in_specs=[in_hbm] * 7,
-        out_specs=in_hbm,
+        out_specs=pl.BlockSpec(memory_space=pltpu.VMEM),
         scratch_shapes=[
             pltpu.SMEM(lengths.shape, jnp.int32),
             pltpu.VMEM((rows, query_cols), bf16),
@@ -342,10 +333,8 @@
             pltpu.VMEM((subs, rows, SUB), bf16),
             pltpu.VMEM((subs, rows, SUB), bf16),
             pltpu.VMEM((subs, rows, SUB), f32),
-            pltpu.VMEM((rows, width), bf16),
             dma((6,)),
             dma,
-            dma((subs,)),
             dma((2, n + 2)),
             dma((2, n)),
             dma((2,)),

time: 38.8 us -> 37.1 us (0.956)
  local copies, waits for them, and re-layouts: 1.87 us -> 0.8 us
  Pallas kernels: 36.7 us -> 36.1 us
    unnamed x1, local copies, waits for them, and re-layouts: 1.87 us -> 0.8 us
    pallas_call x1, Pallas kernels: 36.7 us -> 36.1 us  [local(): pl.pallas_call(functools.partial(kernel, n, n_tp), out_shape=pltpu.VMEM((...]
where the time goes in v3:
time: 37.1 us; the launch traced here: 36.9 us
  Pallas kernels  36.1 us (97%)
  local copies, waits for them, and re-layouts  0.8 us (2%)
    pallas_call x1, Pallas kernels, local(): pl.pallas_call(functools.partial(kernel, n, n_tp), out_shape=pltpu.VMEM((...  36.1 us
    unnamed x1, local copies, waits for them, and re-layouts  0.8 us

profile of v3, /device:TPU:0, one launch (start us, length us, event | category | flops | bytes accessed | tf_op | source)
XLA Modules:
  0.0 36.9 jit_solution(14580432946875879708)
XLA Ops:
  0.0 36.1 %shard_map.73 = bf16[256,1024]{1,0:T(8,128)(2,1)S(1)} custom-call(bf16[256,1024]{1,0:T(8,128)(2,1)} %q_hbm.1, bf16[256,128]{1,0:T(8,128)(2,1)} %rk_hbm.1, bf16[256,128]{1,0:T(8,128)(2,1)} %rv_hbm.1, bf16[256,128]{1,0:T(8,128)(2,1)} %pk_hbm.1, bf16[256,128]{1,0:T(8,128)(2,1)} %pv_hbm.1, s32[6]{0:T(128)} %lengths_hbm.1, bf16[1024,4096]{1,0:T(8,128)(2,1)} %w_hbm.1), custom_call_target="tpu_custom_call" | custom-call | tf_op jit(solution)/shard_map/pallas_call | solution.py:314
  36.1 0.8 %copy.9 = bf16[256,1024]{1,0:T(8,128)(2,1)} copy(bf16[256,1024]{1,0:T(8,128)(2,1)S(1)} %shard_map.73) | data formatting | bytes 1048576

commit v4 on v3

--- a/solution.py
+++ b/solution.py
@@ -152,7 +152,6 @@
                 s = lax.dot_general(
                     query, keys[...], (((1,), (1,)), ((), ())), preferred_element_type=jnp.float32
                 )
-                s = s * SCALE
                 if extra is not None:
                     s = s + extra[...]
                 scores.append(s)
@@ -164,13 +163,13 @@
                 top = jnp.maximum(top, before)
             added = None
             for s, (_, values, _) in zip(scores, parts):
-                p = jnp.exp2(s - top).astype(jnp.bfloat16)
+                p = jnp.exp2((s - top) * SCALE).astype(jnp.bfloat16)
                 term = jnp.dot(p, extended(values[...]), preferred_element_type=jnp.float32)
                 added = term if added is None else added + term
             if fresh:
                 acc[h] = added
             else:
-                acc[h] = acc[h] * jnp.exp2(before - top) + added
+                acc[h] = acc[h] * jnp.exp2((before - top) * SCALE) + added
             tops[h] = top
 
     attend(

time: 37.1 us -> 36.8 us (level)
  no operation moved by 1% of the time
where the time goes in v4:
time: 36.8 us; the launch traced here: 36.7 us
  Pallas kernels  35.9 us (98%)
  local copies, waits for them, and re-layouts  0.8 us (2%)
    pallas_call x1, Pallas kernels, local(): pl.pallas_call(functools.partial(kernel, n, n_tp), out_shape=pltpu.VMEM((...  35.9 us
    unnamed x1, local copies, waits for them, and re-layouts  0.8 us

profile of v4, /device:TPU:0, one launch (start us, length us, event | category | flops | bytes accessed | tf_op | source)
XLA Modules:
  0.0 36.7 jit_solution(4727323948352283852)
XLA Ops:
  0.0 35.9 %shard_map.73 = bf16[256,1024]{1,0:T(8,128)(2,1)S(1)} custom-call(bf16[256,1024]{1,0:T(8,128)(2,1)} %q_hbm.1, bf16[256,128]{1,0:T(8,128)(2,1)} %rk_hbm.1, bf16[256,128]{1,0:T(8,128)(2,1)} %rv_hbm.1, bf16[256,128]{1,0:T(8,128)(2,1)} %pk_hbm.1, bf16[256,128]{1,0:T(8,128)(2,1)} %pv_hbm.1, s32[6]{0:T(128)} %lengths_hbm.1, bf16[1024,4096]{1,0:T(8,128)(2,1)} %w_hbm.1), custom_call_target="tpu_custom_call" | custom-call | tf_op jit(solution)/shard_map/pallas_call | solution.py:313
  35.9 0.8 %copy.9 = bf16[256,1024]{1,0:T(8,128)(2,1)} copy(bf16[256,1024]{1,0:T(8,128)(2,1)S(1)} %shard_map.73) | data formatting | bytes 1048576
